TPU v7x, 32 devices: a whole 2x2x4 slice. The times are simulated.
32 devices in a mesh: tm: 4 (over y, core), panel: 8 (over z, x).
Axes of the slice: x: 2, y: 2, z: 4, core: 2. Of those that a mesh axis runs over, the one named last changes fastest.
Arguments:
- pressure: float32 [4096, 16384], P('tm', 'panel'), may hold values from -6 to 6
- freq_bins: int32 [64], replicated, may hold values from 1 to 2047
- stencil_ids: int32 [4096, 16], P('panel'), may hold values from 0 to 2047
- spline_weights: float32 [4096, 16], P('panel'), may hold values from -2 to 2
- mode_forces: float32 [32, 4096], P(None, 'panel'), may hold values from -0.09375 to 0.09375
- mode_washes: float32 [32, 4096], P(None, 'panel'), may hold values from -6 to 6
Outputs:
- grams: float32 [2, 64, 32, 32], replicated
Inputs may be any that keep to these rules, and one draw needn't show every extreme that they name: `freq_bins`: frequency bins of the excitation lines, possibly repeated. `stencil_ids`: indices within the point group of the panel, group p // 512.
All inputs are finite; a program needn't handle non-finite values.
Results may differ from a plain program's by a relative error of at most 0.000073.
Values sent between devices are 32-bit elements; how exact they have to be, the bound alone decides.
A program may use at most 64 MiB of HBM per device.

v0:
```python
import math

import jax
import jax.numpy as jnp
from jax import lax
from jax.sharding import PartitionSpec as P


def dft_table(freq_bins, first, length, total):
    times = first + jnp.arange(length, dtype=jnp.int32)
    phase = freq_bins[:, None] * times[None, :] % total
    angle = 2.0 * math.pi / total * phase.astype(jnp.float32)
    scale_value = 1.0 / math.sqrt(total)
    return jnp.concatenate([jnp.cos(angle), -jnp.sin(angle)], axis=0) * scale_value


def modal_matrices(panel_spectra, forces_own, washes_own):
    weighted = panel_spectra[:, None, :] * forces_own[None, :, :]
    return lax.dot_general(
        weighted,
        washes_own,
        (((2,), (1,)), ((), ())),
        precision=lax.Precision.HIGHEST,
        preferred_element_type=jnp.float32,
    )


def spline_basis(point_ids, stencil_ids, spline_weights):

    def add_column(column, basis):
        ids_column = lax.dynamic_slice_in_dim(stencil_ids, column, 1, 1)[:, 0]
        weight_column = lax.dynamic_slice_in_dim(spline_weights, column, 1, 1)[:, 0]
        hits = point_ids[:, None] == ids_column[None, :]
        return basis + jnp.where(hits, weight_column[None, :], jnp.float32(0.0))

    start_basis = jnp.zeros((point_ids.shape[0], stencil_ids.shape[0]), jnp.float32)
    return lax.fori_loop(0, stencil_ids.shape[1], add_column, start_basis)


def body(pressure, freq_bins, stencil_ids, spline_weights, mode_forces, mode_washes):
    tm_count = lax.axis_size("tm")
    steps_local = pressure.shape[0]
    steps_total = steps_local * tm_count
    points_local = pressure.shape[1] // tm_count
    point_ids = lax.axis_index("tm") * points_local + jnp.arange(points_local, dtype=jnp.int32)
    local_table = dft_table(freq_bins, lax.axis_index("tm") * steps_local, steps_local, steps_total)
    spectra_rows = lax.psum_scatter(
        lax.dot_general(
            pressure,
            local_table,
            (((0,), (1,)), ((), ())),
            precision=lax.Precision.HIGHEST,
            preferred_element_type=jnp.float32,
        ),
        "tm",
        scatter_dimension=0,
        tiled=True,
    )
    basis = spline_basis(point_ids, stencil_ids, spline_weights)
    partial_spectra = lax.dot_general(
        spectra_rows,
        basis,
        (((0,), (0,)), ((), ())),
        precision=lax.Precision.HIGHEST,
        preferred_element_type=jnp.float32,
    )
    owned = lax.psum_scatter(partial_spectra, "tm", scatter_dimension=1, tiled=True)
    owned_width = owned.shape[1]
    begin = lax.axis_index("tm") * owned_width
    forces_own = lax.dynamic_slice_in_dim(mode_forces, begin, owned_width, 1)
    washes_own = lax.dynamic_slice_in_dim(mode_washes, begin, owned_width, 1)
    local_grams = modal_matrices(owned, forces_own, washes_own)
    summed = lax.psum(local_grams, ("tm", "panel"))
    modes = mode_forces.shape[0]
    return summed.reshape(2, -1, modes, modes)


def solution(mesh):
    placed = (
        P("tm", "panel"),
        P(),
        P("panel", None),
        P("panel", None),
        P(None, "panel"),
        P(None, "panel"),
    )
    return jax.shard_map(body, mesh=mesh, in_specs=placed, out_specs=P(), check_vma=False)
```

profile of v0, /device:TPU:0, one launch (start us, length us, event | category | flops | bytes accessed | tf_op | source)
XLA Modules:
  0.0 212.8 jit_solution(4548003467514517349)
XLA Ops:
  6.5 1.8 fusion.12
  8.3 7.8 %convolution_bitcast_fusion = f32[2048,128]{0,1:T(8,128)} fusion(f32[1024,2048]{1,0:T(8,128)} %param.8, f32[64,1024]{1,0:T(8,128)S(1)} %get-tuple-element.132, f32[64,1024]{1,0:T(8,128)S(1)} %get-tuple-element.131), kind=kOutput, calls=%fused_computation.5 | convolution fusion | flops 3221487616 | bytes 9961472 | tf_op jit(solution)/shard_map/dot_general | solution.py:48
  16.3 27.4 %while.14 = (s32[]{:T(128)}, f32[512,512]{1,0:T(8,128)S(1)}, s32[512,16]{0,1:T(8,128)}, f32[512,16]{0,1:T(8,128)}, s32[]{:T(128)}, /*index=5*/s32[]{:T(128)}, s32[]{:T(128)}) while((s32[]{:T(128)}, f32[512,512]{1,0:T(8,128)S(1)}, s32[512,16]{0,1:T(8,128)}, f32[512,16]{0,1:T(8,128)}, s32[]{:T(128)}, /*index=5*/s32[]{:T(128)}, ...), condition=%wide.region_2.3_spmd.clone, body=%wide.region_1.2_spmd.clone.sunk | while | flops 1049091 | bytes 2113643 | solution.py:37
  16.3 0.7 constant_dynamic-slice_fusion.5
  18.0 0.7 constant_dynamic-slice_fusion.5
  18.7 0.7 constant_dynamic-slice_fusion.6
  19.7 0.7 constant_dynamic-slice_fusion.5
  21.4 0.7 constant_dynamic-slice_fusion.5
  23.1 0.7 constant_dynamic-slice_fusion.5
  23.8 0.7 constant_dynamic-slice_fusion.6
  24.8 0.7 constant_dynamic-slice_fusion.5
  25.6 0.7 constant_dynamic-slice_fusion.6
  26.5 0.7 constant_dynamic-slice_fusion.5
  27.3 0.7 constant_dynamic-slice_fusion.6
  28.3 0.7 constant_dynamic-slice_fusion.5
  30.0 0.7 constant_dynamic-slice_fusion.5
  31.7 0.7 constant_dynamic-slice_fusion.5
  33.4 0.7 constant_dynamic-slice_fusion.5
  35.1 0.7 constant_dynamic-slice_fusion.5
  36.8 0.7 constant_dynamic-slice_fusion.5
  38.5 0.7 constant_dynamic-slice_fusion.5
  39.2 0.7 constant_dynamic-slice_fusion.6
  40.2 0.7 constant_dynamic-slice_fusion.5
  41.0 0.7 constant_dynamic-slice_fusion.6
  41.9 0.7 constant_dynamic-slice_fusion.5
  43.9 2.4 %fusion.18 = f32[128,512]{1,0:T(8,128)} fusion(f32[512,128]{0,1:T(8,128)} %reduce-scatter.3.cloned.1.call-done, f32[512,512]{1,0:T(8,128)S(1)} %get-tuple-element.99), kind=kOutput, calls=%fused_computation.31 | convolution fusion | flops 402653184 | bytes 1572864 | tf_op jit(solution)/shard_map/dot_general | solution.py:60
  46.4 0.7 constant_dynamic-slice_fusion.2
  47.1 21.8 %reduce-scatter.5.cloned.1.call-done = f32[128,128]{1,0:T(8,128)} async-done(((f32[128,512]{1,0:T(8,128)}), f32[128,128]{1,0:T(8,128)}) %reduce-scatter.5.cloned.1.call-update) | async-done | bytes 65552 | tf_op jit(solution)/shard_map/reduce_scatter | solution.py:67
  68.9 3.1 %fusion.2 = f32[128,32,32]{0,2,1:T(8,128)S(1)} fusion(f32[32,128]{1,0:T(8,128)S(1)} %constant_dynamic-slice_fusion.2, f32[128,128]{1,0:T(8,128)} %reduce-scatter.5.cloned.1.call-done, f32[32,512]{1,0:T(8,128)S(1)} %copy-done, s32[]{:T(128)S(6)} %select_n.26), kind=kOutput, calls=%fused_computation.6 | convolution fusion | flops 201850880 | bytes 622596 | tf_op jit(solution)/shard_map/dot_general | solution.py:19
  72.6 1.1 copy.7
  73.8 130.2 %all-reduce.2.cloned.1.call-done = f32[2,64,32,32]{1,3,2,0:T(8,128)} async-done(((f32[2,64,32,32]{1,3,2,0:T(8,128)}), f32[2,64,32,32]{1,3,2,0:T(8,128)}) %all-reduce.2.cloned.1.call-update) | async-done | bytes 524304 | tf_op jit(solution)/shard_map/psum | solution.py:73
  204.0 2.3 %copy.15 = f32[2,64,32,32]{1,3,2,0:T(8,128)} copy(f32[2,64,32,32]{1,3,2,0:T(8,128)} %all-reduce.2.cloned.1.call-done) | data formatting | bytes 1048576
  (54 shorter events, 12.0 us)
Async XLA Ops:
  6.5 62.4 %copy-start = (f32[32,512]{1,0:T(8,128)S(1)}, f32[32,512]{1,0:T(8,128)}, u32[]{:S(2)}) copy-start(f32[32,512]{1,0:T(8,128)} %param.13) | copy-start | bytes 196612
  6.5 37.4 %reduce-scatter.3.cloned.1.call-start = ((), (), s32[]{:S(2)}) async-start(), calls=%async_computation.2 | async-start | bytes 1310720 | tf_op jit(solution)/shard_map/reduce_scatter | solution.py:47
  16.2 52.7 %reduce-scatter.5.cloned.1.call-start = ((), (), s32[]{:S(2)}) async-start(), calls=%async_computation.3 | async-start | bytes 327680 | tf_op jit(solution)/shard_map/reduce_scatter | solution.py:67
  46.3 157.7 %all-reduce.2.cloned.1.call-start = ((), (), s32[]{:S(2)}) async-start(), calls=%async_computation.4 | async-start | bytes 2097152 | tf_op jit(solution)/shard_map/psum | solution.py:73
Sparse Core Ops, SparseCore 0:
  16.3 27.5 reduce-scatter.2
  46.5 22.3 reduce-scatter.4
  74.1 129.8 all-reduce.1
where the time goes:
time: 216 us; the launch traced here: 213 us
  waiting for transfers between devices  152 us (70%)
  local copies, waits for them, and re-layouts  27.9 us (13%)
  matrix products  13.3 us (6%)
  between operations  13.1 us (6%)
  other arithmetic  5.54 us (3%)
    psum x1, waiting for transfers between devices, body(): summed = lax.psum(local_grams, ('tm', 'panel'))  130 us
    reduce_scatter x1, waiting for transfers between devices, body(): lax.psum_scatter(partial_spectra, 'tm', scatter_dimension=1, tiled=True)  21.8 us
    dynamic_slice x16, local copies, waits for them, and re-layouts, add_column(): weight_column = lax.dynamic_slice_in_dim(spline_weights, column, 1, 1)[:, 0]  11.6 us
    dynamic_slice x16, local copies, waits for them, and re-layouts, add_column(): ids_column = lax.dynamic_slice_in_dim(stencil_ids, column, 1, 1)[:, 0]  11.6 us
    dot_general x1, matrix products, body(): lax.dot_general(pressure, local_table, (((0,), (1,)), ((), ())), precisio...  7.85 us
  transfers between devices with their start and end apart: 3, of which 3 were waited for; matrix products, arithmetic and copies ran while one was open for 13% of the time, Pallas kernels for 0%

commit v1 on v0

v1 whole, which is shorter than its diff:
```python
import functools
import math

import jax
import jax.numpy as jnp
from jax import lax
from jax.experimental import pallas as pl
from jax.experimental.pallas import tpu as pltpu
from jax.sharding import PartitionSpec as P

F32 = jnp.float32
BF16 = jnp.bfloat16
LANES = 128
CHUNK = 256
MESH = pl.DeviceIdType.MESH


def split_pair(value):
    high = value.astype(BF16)
    return high, (value - high.astype(F32)).astype(BF16)


def dot_rows(left, right):
    return lax.dot_general(left, right, (((1,), (0,)), ((), ())), preferred_element_type=F32)


def dot_lanes(left, right):
    return lax.dot_general(left, right, (((1,), (1,)), ((), ())), preferred_element_type=F32)


def fill_table(freq_ref, table_ref, first, total):
    freqs = freq_ref.shape[1]
    steps = table_ref.shape[1]
    quarter = total // 4
    spread = jnp.broadcast_to(freq_ref[...].astype(F32), (freqs, freqs))
    on_diagonal = lax.broadcasted_iota(jnp.int32, (freqs, freqs), 0) == lax.broadcasted_iota(
        jnp.int32, (freqs, freqs), 1
    )
    column = jnp.sum(jnp.where(on_diagonal, spread, 0.0), axis=1, keepdims=True).astype(jnp.int32)
    scale = 1.0 / math.sqrt(total)
    width = 2 * LANES

    def fill(block, carry):
        at = pl.multiple_of(block * width, width)
        times = lax.broadcasted_iota(jnp.int32, (freqs, width), 1) + (first + at)
        phase = (column * times) & (total - 1)
        turn = (phase + quarter // 2) >> (quarter.bit_length() - 1)
        x = (phase - turn * quarter).astype(F32) * (2.0 * math.pi / total)
        z = x * x
        sine = x + x * z * (-1.6666654611e-1 + z * (8.3321608736e-3 + z * -1.9515295891e-4))
        cosine = 1.0 - 0.5 * z + z * z * (
            4.166664568298827e-2 + z * (-1.388731625493765e-3 + z * 2.443315711809948e-5)
        )
        odd = (turn & 1) == 1
        cos_raw = jnp.where(odd, sine, cosine)
        sin_raw = jnp.where(odd, cosine, sine)
        cos_sign = jnp.where(((turn + 1) & 2) == 2, -scale, scale)
        sin_sign = jnp.where((turn & 2) == 2, scale, -scale)
        cos_high, cos_low = split_pair(cos_raw * cos_sign)
        sin_high, sin_low = split_pair(sin_raw * sin_sign)
        for place, part in enumerate((cos_high, sin_high, cos_low, sin_low)):
            table_ref[place * freqs:(place + 1) * freqs, pl.ds(at, width)] = part
        return carry

    lax.fori_loop(0, steps // width, fill, 0)


def fill_stencils(ids_ref, weights_ref, ids_rows, high_rows, low_rows):
    ids = ids_ref[...]
    weights = weights_ref[...]
    count = ids.shape[0]
    merged = weights
    for shift in range(1, count):
        same = pltpu.roll(ids, shift, 0) == ids
        merged = merged + jnp.where(same, pltpu.roll(weights, shift, 0), 0.0)
    high, low = split_pair(merged)
    high = high.astype(F32)
    low = low.astype(F32)
    for k in range(count):
        rows = slice(16 * k, 16 * k + 16)
        full = (16, ids.shape[1])
        ids_rows[rows, :] = jnp.broadcast_to(ids[k:k + 1, :], full).astype(jnp.int16)
        high_rows[rows, :] = jnp.broadcast_to(high[k:k + 1, :], full).astype(BF16)
        low_rows[rows, :] = jnp.broadcast_to(low[k:k + 1, :], full).astype(BF16)


def fill_basis(base, points, ids_rows, high_rows, low_rows, basis_high, basis_low):
    count = ids_rows.shape[0] // 16
    group = 8
    for half in range(points // (16 * group)):
        rows_at = [half * 16 * group + 16 * g for g in range(group)]
        wanted = [
            (lax.broadcasted_iota(jnp.int32, (16, LANES), 0) + (base + at)).astype(jnp.int16) for at in rows_at
        ]
        for tile in range(ids_rows.shape[1] // LANES):
            lanes = slice(tile * LANES, (tile + 1) * LANES)
            high = [jnp.zeros((16, LANES), BF16)] * group
            low = [jnp.zeros((16, LANES), BF16)] * group
            for k in range(count):
                rows = slice(16 * k, 16 * k + 16)
                ids_k = ids_rows[rows, lanes]
                high_k = high_rows[rows, lanes]
                low_k = low_rows[rows, lanes]
                for g in range(group):
                    hit = wanted[g] == ids_k
                    high[g] = jnp.where(hit, high_k, high[g])
                    low[g] = jnp.where(hit, low_k, low[g])
            for g in range(group):
                basis_high[rows_at[g]:rows_at[g] + 16, lanes] = high[g]
                basis_low[rows_at[g]:rows_at[g] + 16, lanes] = low[g]


def fill_products(forces_ref, washes_ref, high_ref, low_ref):
    modes = forces_ref.shape[0]

    def fill(m, carry):
        at = pl.multiple_of(m * modes, modes)
        high, low = split_pair(forces_ref[pl.ds(m, 1), :] * washes_ref[...])
        high_ref[pl.ds(at, modes), :] = high
        low_ref[pl.ds(at, modes), :] = low
        return carry

    lax.fori_loop(0, modes, fill, 0)


def kernel(
    tm_count, panel_count,
    pressure_ref, freq_in, ids_in, weights_in, forces_in, washes_in,
    out_ref,
    freq_ref, ids_ref, weights_ref, forces_ref, washes_ref,
    pressure_buf, table, ids_rows, high_rows, low_rows, basis_high, basis_low,
    partial, first_buf, product_high, product_low, local, second_buf, gathered,
    small_sem, load_sem, first_send, first_recv, second_send, second_recv,
    wide_send, wide_recv, core_send, core_recv, side_send, side_recv, last_send, last_recv,
):
    me_t = lax.axis_index("tm")
    me_p = lax.axis_index("panel")
    core = lax.rem(me_t, 2)
    side = me_t // 2
    sides = tm_count // 2

    def tm_at(rel):
        return 2 * lax.rem(side + rel // 2, sides) + lax.rem(core + rel % 2, 2)

    rels = range(1, tm_count)
    partner = tm_at(1)
    steps, points = pressure_ref.shape
    chunks = points // CHUNK
    cells = partial.shape[0]
    own_rows = cells // tm_count
    rows = local.shape[1]
    bands = own_rows // rows
    blocks = panel_count // bands

    def load(j):
        return pltpu.make_async_copy(
            pressure_ref.at[:, pl.ds(pl.multiple_of(j * CHUNK, CHUNK), CHUNK)], pressure_buf.at[j], load_sem.at[j]
        )

    small = [
        pltpu.make_async_copy(source, target, small_sem.at[place])
        for place, (source, target) in enumerate((
            (freq_in, freq_ref), (ids_in, ids_ref), (weights_in, weights_ref),
            (forces_in, forces_ref), (washes_in, washes_ref),
        ))
    ]
    for copy in small:
        copy.start()
    for j in range(chunks):
        load(j).start()

    barrier = pltpu.get_barrier_semaphore()
    for rel in rels:
        pl.semaphore_signal(barrier, inc=1, device_id=(tm_at(rel), me_p), device_id_type=MESH)
    for d in range(1, panel_count):
        pl.semaphore_signal(
            barrier, inc=1, device_id=(me_t, lax.rem(me_p + d, panel_count)), device_id_type=MESH
        )

    small[0].wait()
    fill_table(freq_ref, table, me_t * steps, steps * tm_count)
    small[1].wait()
    small[2].wait()
    fill_stencils(ids_ref, weights_ref, ids_rows, high_rows, low_rows)
    partial[...] = jnp.zeros_like(partial)

    def chunk_step(j, carry):
        load(j).wait()
        block_high, block_low = split_pair(pressure_buf[j])
        wide = dot_rows(table[...], block_high)
        spectra = wide[:cells] + wide[cells:] + dot_rows(table[:cells, :], block_low)
        fill_basis(j * CHUNK, CHUNK, ids_rows, high_rows, low_rows, basis_high, basis_low)
        spectra_high, spectra_low = split_pair(spectra)
        partial[...] += (
            dot_rows(spectra_high, basis_high[...])
            + dot_rows(spectra_low, basis_high[...])
            + dot_rows(spectra_high, basis_low[...])
        )
        return carry

    lax.fori_loop(0, chunks, chunk_step, 0)

    pl.semaphore_wait(barrier, tm_count + panel_count - 2)

    first = {}
    for rel in reversed(rels):
        first[rel] = pltpu.make_async_remote_copy(
            src_ref=partial.at[pl.ds(pl.multiple_of(tm_at(rel) * own_rows, own_rows), own_rows)],
            dst_ref=first_buf.at[rel - 1],
            send_sem=first_send.at[rel - 1],
            recv_sem=first_recv.at[rel - 1],
            device_id=(tm_at(rel), me_p),
            device_id_type=MESH,
        )
        first[rel].start()
    small[3].wait()
    small[4].wait()
    fill_products(forces_ref, washes_ref, product_high, product_low)
    owned = partial[pl.ds(pl.multiple_of(me_t * own_rows, own_rows), own_rows), :]
    for rel in rels:
        first[rel].wait_recv()
        owned = owned + first_buf[rel - 1]
    owned_high, owned_low = split_pair(owned)
    for pair in range(blocks // 2):
        span = slice(pair * 2 * LANES, (pair + 1) * 2 * LANES)
        grams = (
            dot_lanes(owned_high, product_high[span, :])
            + dot_lanes(owned_low, product_high[span, :])
            + dot_lanes(owned_high, product_low[span, :])
        )
        for part in range(2):
            for band in range(bands):
                local[band * blocks + 2 * pair + part] = grams[
                    band * rows:(band + 1) * rows, part * LANES:(part + 1) * LANES
                ]

    second = []
    for d in range(1, panel_count):
        target = lax.rem(me_p + d, panel_count)
        copy = pltpu.make_async_remote_copy(
            src_ref=local.at[target],
            dst_ref=second_buf.at[d - 1],
            send_sem=second_send.at[d - 1],
            recv_sem=second_recv.at[d - 1],
            device_id=(me_t, target),
            device_id_type=MESH,
        )
        copy.start()
        second.append(copy)
    total = local[me_p]
    for d in range(1, panel_count):
        second[d - 1].wait_recv()
        total = total + second_buf[d - 1]
    gathered[me_t, me_p] = total

    def share(p, t, sends, recvs, index, device):
        place = gathered.at[t, p]
        copy = pltpu.make_async_remote_copy(
            src_ref=place,
            dst_ref=place,
            send_sem=sends.at[index],
            recv_sem=recvs.at[index],
            device_id=device,
            device_id_type=MESH,
        )
        return copy

    wide, to_core, to_side, last = [], [], [], []
    for d in range(1, panel_count):
        copy = share(me_p, me_t, wide_send, wide_recv, d - 1, (me_t, lax.rem(me_p + d, panel_count)))
        copy.start()
        wide.append(copy)
    for d in range(panel_count):
        origin = lax.rem(me_p + panel_count - d, panel_count)
        if d > 0:
            wide[d - 1].wait_recv()
        for hop in range(1, sides):
            copy = share(
                origin, me_t, side_send, side_recv, (hop - 1) * panel_count + d, (tm_at(2 * hop), me_p)
            )
            copy.start()
            to_side.append(copy)
        copy = share(origin, me_t, core_send, core_recv, d, (partner, me_p))
        copy.start()
        to_core.append(copy)
    for d in range(panel_count):
        origin = lax.rem(me_p + panel_count - d, panel_count)
        for hop in range(1, sides):
            to_side[d * (sides - 1) + hop - 1].wait_recv()
            copy = share(
                origin, tm_at(2 * (sides - hop)), last_send, last_recv, (hop - 1) * panel_count + d, (partner, me_p)
            )
            copy.start()
            last.append(copy)
    for copy in to_core + last:
        copy.wait_recv()

    def turn(block, carry):
        at = pl.multiple_of(block * LANES, LANES)
        for c in range(2):
            parts = [
                gathered[t, band * blocks + block]
                for t in range(c * sides, (c + 1) * sides)
                for band in range(bands)
            ]
            out_ref[c, pl.ds(at, LANES), :] = jnp.concatenate(parts, axis=0).T
        return carry

    lax.fori_loop(0, blocks, turn, 0)

    for copy in list(first.values()) + second + wide + to_core + to_side + last:
        copy.wait_send()


def body(pressure, freq_bins, stencil_ids, spline_weights, mode_forces, mode_washes):
    tm_count = lax.axis_size("tm")
    panel_count = lax.axis_size("panel")
    steps, points = pressure.shape
    freqs = freq_bins.shape[0]
    panels, stencil = stencil_ids.shape
    modes = mode_forces.shape[0]
    cells = 2 * freqs
    own_rows = cells // tm_count
    blocks = modes * modes // LANES
    rows = own_rows * blocks // panel_count
    chunks = points // CHUNK
    vmem = pl.BlockSpec(memory_space=pltpu.VMEM)
    peers = panel_count - 1
    far = (tm_count // 2 - 1) * panel_count
    dma = pltpu.SemaphoreType.DMA
    grams = pl.pallas_call(
        functools.partial(kernel, tm_count, panel_count),
        out_shape=jax.ShapeDtypeStruct((2, modes * modes, freqs), F32),
        in_specs=[pl.BlockSpec(memory_space=pl.ANY)] * 6,
        out_specs=vmem,
        scratch_shapes=[
            pltpu.VMEM((1, freqs), jnp.int32),
            pltpu.VMEM((stencil, panels), jnp.int32),
            pltpu.VMEM((stencil, panels), F32),
            pltpu.VMEM((modes, panels), F32),
            pltpu.VMEM((modes, panels), F32),
            pltpu.VMEM((chunks, steps, CHUNK), F32),
            pltpu.VMEM((2 * cells, steps), BF16),
            pltpu.VMEM((16 * stencil, panels), jnp.int16),
            pltpu.VMEM((16 * stencil, panels), BF16),
            pltpu.VMEM((16 * stencil, panels), BF16),
            pltpu.VMEM((CHUNK, panels), BF16),
            pltpu.VMEM((CHUNK, panels), BF16),
            pltpu.VMEM((cells, panels), F32),
            pltpu.VMEM((tm_count - 1, own_rows, panels), F32),
            pltpu.VMEM((modes * modes, panels), BF16),
            pltpu.VMEM((modes * modes, panels), BF16),
            pltpu.VMEM((panel_count, rows, LANES), F32),
            pltpu.VMEM((peers, rows, LANES), F32),
            pltpu.VMEM((tm_count, panel_count, rows, LANES), F32),
            dma((5,)),
            dma((chunks,)),
            dma((tm_count - 1,)), dma((tm_count - 1,)),
            dma((peers,)), dma((peers,)),
            dma((peers,)), dma((peers,)),
            dma((panel_count,)), dma((panel_count,)),
            dma((far,)), dma((far,)),
            dma((far,)), dma((far,)),
        ],
        compiler_params=pltpu.CompilerParams(
            collective_id=0, has_side_effects=True, vmem_limit_bytes=58 * 1024 * 1024
        ),
        cost_estimate=pl.CostEstimate(flops=4 * 10**9, bytes_accessed=10 * 2**20, transcendentals=0),
    )(
        pressure,
        freq_bins.reshape(1, freqs),
        stencil_ids.T,
        spline_weights.T,
        mode_forces,
        mode_washes,
    )
    return grams.reshape(2, modes, modes, freqs).transpose(0, 3, 1, 2)


def solution(mesh):
    placed = (
        P("tm", "panel"),
        P(),
        P("panel", None),
        P("panel", None),
        P(None, "panel"),
        P(None, "panel"),
    )
    return jax.shard_map(body, mesh=mesh, in_specs=placed, out_specs=P(), check_vma=False)
```

time: 216 us -> 41.6 us (0.19)
  the two profiles are of different devices: /device:TPU:0 before, /device:TPU:1 now
where the time goes in v1:
time: 41.6 us; the launch traced here: 41.5 us
  Pallas kernels  39.2 us (94%)
  local copies, waits for them, and re-layouts  2.26 us (5%)
    pallas_call x1, Pallas kernels, body(): pl.pallas_call(functools.partial(kernel, tm_count, panel_count), out_shap...  39.2 us
    unnamed x1, local copies, waits for them, and re-layouts  2.26 us

profile of v1, /device:TPU:1, one launch (start us, length us, event | category | flops | bytes accessed | tf_op | source)
XLA Modules:
  0.0 41.5 jit_solution(6210354761584055573)
XLA Ops:
  0.0 39.2 %shard_map.64 = f32[2,1024,64]{2,1,0:T(8,128)} custom-call(f32[1024,2048]{1,0:T(8,128)} %pressure_ref.1, s32[1,64]{1,0:T(1,128)} %bitcast.9, s32[16,512]{1,0:T(8,128)} %bitcast.7, f32[16,512]{1,0:T(8,128)} %bitcast.8, f32[32,512]{1,0:T(8,128)} %forces_in.1, f32[32,512]{1,0:T(8,128)} %washes_in.1), custom_call_target="tpu_custom_call" | custom-call | flops 4000000000 | bytes 10485760 | tf_op jit(solution)/shard_map/pallas_call | solution.py:331
  39.2 2.3 %copy.8 = f32[2,64,32,32]{1,3,2,0:T(8,128)} copy(f32[2,64,32,32]{1,3,2,0:T(8,128)} %bitcast.6) | data formatting | bytes 1048576

commit v2 on v1

--- a/solution.py
+++ b/solution.py
@@ -11,7 +11,7 @@
 F32 = jnp.float32
 BF16 = jnp.bfloat16
 LANES = 128
-CHUNK = 256
+CHUNK = 512
 MESH = pl.DeviceIdType.MESH
 
 
@@ -129,8 +129,9 @@
     out_ref,
     freq_ref, ids_ref, weights_ref, forces_ref, washes_ref,
     pressure_buf, table, ids_rows, high_rows, low_rows, basis_high, basis_low,
+    spectra_out, spectra_in, spectra_own, spectra_high, spectra_low,
     partial, first_buf, product_high, product_low, local, second_buf, gathered,
-    small_sem, load_sem, first_send, first_recv, second_send, second_recv,
+    small_sem, load_sem, swap_send, swap_recv, first_send, first_recv, second_send, second_recv,
     wide_send, wide_recv, core_send, core_recv, side_send, side_recv, last_send, last_recv,
 ):
     me_t = lax.axis_index("tm")
@@ -152,9 +153,22 @@
     bands = own_rows // rows
     blocks = panel_count // bands
 
+    own_chunks = chunks // 2
+
     def load(j):
+        place = lax.rem(j + (1 - core) * own_chunks, chunks)
         return pltpu.make_async_copy(
-            pressure_ref.at[:, pl.ds(pl.multiple_of(j * CHUNK, CHUNK), CHUNK)], pressure_buf.at[j], load_sem.at[j]
+            pressure_ref.at[:, pl.ds(pl.multiple_of(place * CHUNK, CHUNK), CHUNK)], pressure_buf.at[j], load_sem.at[j]
+        )
+
+    def swap(j):
+        return pltpu.make_async_remote_copy(
+            src_ref=spectra_out.at[j],
+            dst_ref=spectra_in.at[j],
+            send_sem=swap_send.at[j],
+            recv_sem=swap_recv.at[j],
+            device_id=(partner, me_p),
+            device_id_type=MESH,
         )
 
     small = [
@@ -182,25 +196,47 @@
     small[1].wait()
     small[2].wait()
     fill_stencils(ids_ref, weights_ref, ids_rows, high_rows, low_rows)
-    partial[...] = jnp.zeros_like(partial)
-
-    def chunk_step(j, carry):
+
+    def basis_step(j, carry):
+        at = pl.multiple_of(j * LANES, LANES)
+        fill_basis(
+            core * own_chunks * CHUNK + at, LANES, ids_rows, high_rows, low_rows,
+            basis_high.at[pl.ds(at, LANES)], basis_low.at[pl.ds(at, LANES)],
+        )
+        return carry
+
+    lax.fori_loop(0, own_chunks * CHUNK // LANES, basis_step, 0)
+
+    def transform(j):
         load(j).wait()
         block_high, block_low = split_pair(pressure_buf[j])
         wide = dot_rows(table[...], block_high)
-        spectra = wide[:cells] + wide[cells:] + dot_rows(table[:cells, :], block_low)
-        fill_basis(j * CHUNK, CHUNK, ids_rows, high_rows, low_rows, basis_high, basis_low)
-        spectra_high, spectra_low = split_pair(spectra)
-        partial[...] += (
-            dot_rows(spectra_high, basis_high[...])
-            + dot_rows(spectra_low, basis_high[...])
-            + dot_rows(spectra_high, basis_low[...])
-        )
-        return carry
-
-    lax.fori_loop(0, chunks, chunk_step, 0)
+        return wide[:cells] + wide[cells:] + dot_rows(table[:cells, :], block_low)
 
     pl.semaphore_wait(barrier, tm_count + panel_count - 2)
+
+    def other_step(j, carry):
+        spectra_out[j] = transform(j)
+        swap(j).start()
+        return carry
+
+    def own_step(j, carry):
+        spectra_own[j] = transform(own_chunks + j)
+        return carry
+
+    lax.fori_loop(0, own_chunks, other_step, 0)
+    lax.fori_loop(0, own_chunks, own_step, 0)
+    for j in range(own_chunks):
+        swap(j).wait_recv()
+        high, low = split_pair(spectra_own[j] + spectra_in[j])
+        span = slice(j * CHUNK, (j + 1) * CHUNK)
+        spectra_high[:, span] = high
+        spectra_low[:, span] = low
+    partial[...] = (
+        dot_rows(spectra_high[...], basis_high[...])
+        + dot_rows(spectra_low[...], basis_high[...])
+        + dot_rows(spectra_high[...], basis_low[...])
+    )
 
     first = {}
     for rel in reversed(rels):
@@ -308,6 +344,8 @@
 
     lax.fori_loop(0, blocks, turn, 0)
 
+    for j in range(own_chunks):
+        swap(j).wait_send()
     for copy in list(first.values()) + second + wide + to_core + to_side + last:
         copy.wait_send()
 
@@ -331,7 +369,7 @@
     grams = pl.pallas_call(
         functools.partial(kernel, tm_count, panel_count),
         out_shape=jax.ShapeDtypeStruct((2, modes * modes, freqs), F32),
-        in_specs=[pl.BlockSpec(memory_space=pl.ANY)] * 6,
+        in_specs=[pl.BlockSpec(memory_space=pltpu.HBM)] * 6,
         out_specs=vmem,
         scratch_shapes=[
             pltpu.VMEM((1, freqs), jnp.int32),
@@ -344,8 +382,13 @@
             pltpu.VMEM((16 * stencil, panels), jnp.int16),
             pltpu.VMEM((16 * stencil, panels), BF16),
             pltpu.VMEM((16 * stencil, panels), BF16),
-            pltpu.VMEM((CHUNK, panels), BF16),
-            pltpu.VMEM((CHUNK, panels), BF16),
+            pltpu.VMEM((points // 2, panels), BF16),
+            pltpu.VMEM((points // 2, panels), BF16),
+            pltpu.VMEM((chunks // 2, cells, CHUNK), F32),
+            pltpu.VMEM((chunks // 2, cells, CHUNK), F32),
+            pltpu.VMEM((chunks // 2, cells, CHUNK), F32),
+            pltpu.VMEM((cells, points // 2), BF16),
+            pltpu.VMEM((cells, points // 2), BF16),
             pltpu.VMEM((cells, panels), F32),
             pltpu.VMEM((tm_count - 1, own_rows, panels), F32),
             pltpu.VMEM((modes * modes, panels), BF16),
@@ -355,6 +398,7 @@
             pltpu.VMEM((tm_count, panel_count, rows, LANES), F32),
             dma((5,)),
             dma((chunks,)),
+            dma((chunks // 2,)), dma((chunks // 2,)),
             dma((tm_count - 1,)), dma((tm_count - 1,)),
             dma((peers,)), dma((peers,)),
             dma((peers,)), dma((peers,)),
@@ -363,16 +407,16 @@
             dma((far,)), dma((far,)),
         ],
         compiler_params=pltpu.CompilerParams(
-            collective_id=0, has_side_effects=True, vmem_limit_bytes=58 * 1024 * 1024
+            collective_id=0, has_side_effects=True, vmem_limit_bytes=50 * 1024 * 1024
         ),
         cost_estimate=pl.CostEstimate(flops=4 * 10**9, bytes_accessed=10 * 2**20, transcendentals=0),
     )(
-        pressure,
-        freq_bins.reshape(1, freqs),
-        stencil_ids.T,
-        spline_weights.T,
-        mode_forces,
-        mode_washes,
+        *(
+            pltpu.with_memory_space_constraint(array, pltpu.HBM)
+            for array in (
+                pressure, freq_bins.reshape(1, freqs), stencil_ids.T, spline_weights.T, mode_forces, mode_washes
+            )
+        )
     )
     return grams.reshape(2, modes, modes, freqs).transpose(0, 3, 1, 2)
 

time: 41.6 us -> 32.8 us (0.79)
  Pallas kernels: 39.2 us -> 31.6 us
  local copies, waits for them, and re-layouts: 2.26 us -> 0.97 us
    pallas_call x1, Pallas kernels: 39.2 us -> 31.6 us  [body(): pl.pallas_call(functools.partial(kernel, tm_count, panel_count), out_shap...]
    unnamed x1, local copies, waits for them, and re-layouts: 2.26 us -> 0.97 us
where the time goes in v2:
time: 32.8 us; the launch traced here: 32.6 us
  Pallas kernels  31.6 us (96%)
  local copies, waits for them, and re-layouts  0.97 us (3%)
    pallas_call x1, Pallas kernels, body(): pl.pallas_call(functools.partial(kernel, tm_count, panel_count), out_shap...  31.6 us
    unnamed x1, local copies, waits for them, and re-layouts  0.97 us

profile of v2, /device:TPU:1, one launch (start us, length us, event | category | flops | bytes accessed | tf_op | source)
XLA Modules:
  0.0 32.6 jit_solution(15812769348809125092)
XLA Ops:
  0.0 31.6 %shard_map.64 = f32[2,1024,64]{2,1,0:T(8,128)S(1)} custom-call(f32[1024,2048]{1,0:T(8,128)} %pressure_ref.1, s32[1,64]{1,0:T(1,128)} %bitcast.9, s32[16,512]{1,0:T(8,128)} %bitcast.7, f32[16,512]{1,0:T(8,128)} %bitcast.8, f32[32,512]{1,0:T(8,128)} %forces_in.1, f32[32,512]{1,0:T(8,128)} %washes_in.1), custom_call_target="tpu_custom_call" | custom-call | flops 4000000000 | bytes 10485760 | tf_op jit(solution)/shard_map/pallas_call | solution.py:369
  31.6 1.0 %copy.8 = f32[2,64,32,32]{1,3,2,0:T(8,128)} copy(f32[2,64,32,32]{1,3,2,0:T(8,128)S(1)} %bitcast.6) | data formatting | bytes 1048576

commit v3 on v2

--- a/solution.py
+++ b/solution.py
@@ -270,61 +270,76 @@
                     band * rows:(band + 1) * rows, part * LANES:(part + 1) * LANES
                 ]
 
-    second = []
-    for d in range(1, panel_count):
-        target = lax.rem(me_p + d, panel_count)
-        copy = pltpu.make_async_remote_copy(
-            src_ref=local.at[target],
-            dst_ref=second_buf.at[d - 1],
-            send_sem=second_send.at[d - 1],
-            recv_sem=second_recv.at[d - 1],
-            device_id=(me_t, target),
+    owners = panel_count // 2
+    lowest = panel_count // 4
+    mine = me_p - lowest
+    is_owner = jnp.logical_and(mine >= 0, mine < owners)
+    base = jnp.minimum(jnp.maximum(mine, 0), owners - 1)
+
+    def reduce_to(q, slot):
+        return pltpu.make_async_remote_copy(
+            src_ref=local.at[pl.ds(2 * q, 2)],
+            dst_ref=second_buf.at[slot],
+            send_sem=second_send.at[q],
+            recv_sem=second_recv.at[slot],
+            device_id=(me_t, lowest + q),
             device_id_type=MESH,
         )
-        copy.start()
-        second.append(copy)
-    total = local[me_p]
-    for d in range(1, panel_count):
-        second[d - 1].wait_recv()
-        total = total + second_buf[d - 1]
-    gathered[me_t, me_p] = total
-
-    def share(p, t, sends, recvs, index, device):
-        place = gathered.at[t, p]
-        copy = pltpu.make_async_remote_copy(
-            src_ref=place,
-            dst_ref=place,
-            send_sem=sends.at[index],
-            recv_sem=recvs.at[index],
-            device_id=device,
-            device_id_type=MESH,
-        )
-        return copy
-
-    wide, to_core, to_side, last = [], [], [], []
-    for d in range(1, panel_count):
-        copy = share(me_p, me_t, wide_send, wide_recv, d - 1, (me_t, lax.rem(me_p + d, panel_count)))
-        copy.start()
-        wide.append(copy)
-    for d in range(panel_count):
-        origin = lax.rem(me_p + panel_count - d, panel_count)
-        if d > 0:
-            wide[d - 1].wait_recv()
+
+    def share(q, t, send, recv, device):
+        place = gathered.at[t, pl.ds(2 * q, 2)]
+        return pltpu.make_async_remote_copy(
+            src_ref=place, dst_ref=place, send_sem=send, recv_sem=recv, device_id=device, device_id_type=MESH
+        )
+
+    def spread(p):
+        return share(base, me_t, wide_send.at[p], wide_recv.at[base], (me_t, p))
+
+    for q in range(owners):
+        @pl.when(me_p != lowest + q)
+        def _():
+            reduce_to(q, me_p).start()
+
+    @pl.when(is_owner)
+    def _():
+        total = local[pl.ds(2 * base, 2)]
+        second_buf[me_p] = total
+        for p in range(panel_count):
+            @pl.when(me_p != p)
+            def _():
+                reduce_to(base, p).wait_recv()
+        total = second_buf[0]
+        for p in range(1, panel_count):
+            total = total + second_buf[p]
+        gathered[me_t, pl.ds(2 * base, 2)] = total
+        for p in range(panel_count):
+            @pl.when(me_p != p)
+            def _():
+                spread(p).start()
+
+    to_core, to_side, last = [], [], []
+    for step in range(owners):
+        q = lax.rem(base + step, owners)
+
+        @pl.when(me_p != lowest + q)
+        def _():
+            share(q, me_t, wide_send.at[me_p], wide_recv.at[q], (me_t, lowest + q)).wait_recv()
+
         for hop in range(1, sides):
-            copy = share(
-                origin, me_t, side_send, side_recv, (hop - 1) * panel_count + d, (tm_at(2 * hop), me_p)
-            )
+            at = (hop - 1) * owners + step
+            copy = share(q, me_t, side_send.at[at], side_recv.at[at], (tm_at(2 * hop), me_p))
             copy.start()
             to_side.append(copy)
-        copy = share(origin, me_t, core_send, core_recv, d, (partner, me_p))
+        copy = share(q, me_t, core_send.at[step], core_recv.at[step], (partner, me_p))
         copy.start()
         to_core.append(copy)
-    for d in range(panel_count):
-        origin = lax.rem(me_p + panel_count - d, panel_count)
+    for step in range(owners):
+        q = lax.rem(base + step, owners)
         for hop in range(1, sides):
-            to_side[d * (sides - 1) + hop - 1].wait_recv()
+            at = (hop - 1) * owners + step
+            to_side[step * (sides - 1) + hop - 1].wait_recv()
             copy = share(
-                origin, tm_at(2 * (sides - hop)), last_send, last_recv, (hop - 1) * panel_count + d, (partner, me_p)
+                q, tm_at(2 * (sides - hop)), last_send.at[at], last_recv.at[at], (partner, me_p)
             )
             copy.start()
             last.append(copy)
@@ -346,8 +361,19 @@
 
     for j in range(own_chunks):
         swap(j).wait_send()
-    for copy in list(first.values()) + second + wide + to_core + to_side + last:
+    for copy in list(first.values()) + to_core + to_side + last:
         copy.wait_send()
+    for q in range(owners):
+        @pl.when(me_p != lowest + q)
+        def _():
+            reduce_to(q, me_p).wait_send()
+
+    @pl.when(is_owner)
+    def _():
+        for p in range(panel_count):
+            @pl.when(me_p != p)
+            def _():
+                spread(p).wait_send()
 
 
 def body(pressure, freq_bins, stencil_ids, spline_weights, mode_forces, mode_washes):
@@ -363,8 +389,8 @@
     rows = own_rows * blocks // panel_count
     chunks = points // CHUNK
     vmem = pl.BlockSpec(memory_space=pltpu.VMEM)
-    peers = panel_count - 1
-    far = (tm_count // 2 - 1) * panel_count
+    owners = panel_count // 2
+    far = (tm_count // 2 - 1) * owners
     dma = pltpu.SemaphoreType.DMA
     grams = pl.pallas_call(
         functools.partial(kernel, tm_count, panel_count),
@@ -394,15 +420,15 @@
             pltpu.VMEM((modes * modes, panels), BF16),
             pltpu.VMEM((modes * modes, panels), BF16),
             pltpu.VMEM((panel_count, rows, LANES), F32),
-            pltpu.VMEM((peers, rows, LANES), F32),
+            pltpu.VMEM((panel_count, 2, rows, LANES), F32),
             pltpu.VMEM((tm_count, panel_count, rows, LANES), F32),
             dma((5,)),
             dma((chunks,)),
             dma((chunks // 2,)), dma((chunks // 2,)),
             dma((tm_count - 1,)), dma((tm_count - 1,)),
-            dma((peers,)), dma((peers,)),
-            dma((peers,)), dma((peers,)),
-            dma((panel_count,)), dma((panel_count,)),
+            dma((owners,)), dma((panel_count,)),
+            dma((panel_count,)), dma((owners,)),
+            dma((owners,)), dma((owners,)),
             dma((far,)), dma((far,)),
             dma((far,)), dma((far,)),
         ],

time: 32.8 us -> 31.9 us (0.973)
  Pallas kernels: 31.6 us -> 30.8 us
    pallas_call x1, Pallas kernels: 31.6 us -> 30.8 us  [body(): pl.pallas_call(functools.partial(kernel, tm_count, panel_count), out_shap...]
where the time goes in v3:
time: 31.9 us; the launch traced here: 31.7 us
  Pallas kernels  30.8 us (97%)
  local copies, waits for them, and re-layouts  0.97 us (3%)
    pallas_call x1, Pallas kernels, body(): pl.pallas_call(functools.partial(kernel, tm_count, panel_count), out_shap...  30.8 us
    unnamed x1, local copies, waits for them, and re-layouts  0.97 us

profile of v3, /device:TPU:1, one launch (start us, length us, event | category | flops | bytes accessed | tf_op | source)
XLA Modules:
  0.0 31.7 jit_solution(1086335988525441978)
XLA Ops:
  0.0 30.8 %shard_map.64 = f32[2,1024,64]{2,1,0:T(8,128)S(1)} custom-call(f32[1024,2048]{1,0:T(8,128)} %pressure_ref.1, s32[1,64]{1,0:T(1,128)} %bitcast.9, s32[16,512]{1,0:T(8,128)} %bitcast.7, f32[16,512]{1,0:T(8,128)} %bitcast.8, f32[32,512]{1,0:T(8,128)} %forces_in.1, f32[32,512]{1,0:T(8,128)} %washes_in.1), custom_call_target="tpu_custom_call" | custom-call | flops 4000000000 | bytes 10485760 | tf_op jit(solution)/shard_map/pallas_call | solution.py:395
  30.8 1.0 %copy.8 = f32[2,64,32,32]{1,3,2,0:T(8,128)} copy(f32[2,64,32,32]{1,3,2,0:T(8,128)S(1)} %bitcast.6) | data formatting | bytes 1048576
